TPU v7x, 256 devices: a whole 4x4x8 slice. The times are simulated.
256 devices in a mesh: seq: 32 (over x, z), kvh: 8 (over y, core).
Axes of the slice: x: 4, y: 4, z: 8, core: 2. Of those that a mesh axis runs over, the one named last changes fastest.
Arguments:
- queries: bfloat16 [512, 8192], P('seq', 'kvh'), may hold values from -240 to 240
- trace_cache_keys: bfloat16 [131072, 1024], P('seq', 'kvh'), may hold values from -7 to 7
- trace_cache_values: bfloat16 [131072, 1024], P('seq', 'kvh'), may hold values from -6 to 6
- out_weight: bfloat16 [8192, 8192], P('kvh', 'seq'), may hold values from -0.0625 to 0.0625
- positions: int32 [512], P('seq'), may hold values from 1 to 131072, as said below
- partner: int32 [512], replicated, may hold values from 0 to 511, as said below
Outputs:
- mixed: bfloat16 [512, 8192], P('kvh', 'seq')
- contrast: bfloat16 [512, 8192], P('kvh', 'seq')
Inputs may be any that keep to these rules, and one draw needn't show every extreme that they name: Token t sees trace positions 0 to positions[t] - 1; some token sees all 131072 positions. partner pairs the tokens: partner[partner[t]] = t and partner[t] != t.
All inputs are finite; a program needn't handle non-finite values.
Results may differ from a plain program's by a relative error of at most 0.01.
Values may be sent and summed in bfloat16 or wider, within the bound.
A program may use at most 64 MiB of HBM per device.

v0:
```python
import math

import jax
import jax.numpy as jnp
from jax import lax
from jax.sharding import PartitionSpec as P

QUERY_HEADS = 64
KEY_VALUE_HEADS = 8
HEAD_SIZE = 128


lowest = -1e30


def block_partials(query_rows, key_blk, value_blk, pos_rows, start_pos):
    rows = query_rows.shape[0]
    length = key_blk.shape[0]
    local_kv = key_blk.shape[1] // HEAD_SIZE
    query_group = QUERY_HEADS // KEY_VALUE_HEADS
    grouped_queries = query_rows.reshape(rows, local_kv, query_group, HEAD_SIZE)
    key_heads = key_blk.reshape(length, local_kv, HEAD_SIZE)
    value_heads = value_blk.reshape(length, local_kv, HEAD_SIZE)
    scores = jnp.einsum(
        "tkgd,ckd->tkgc", grouped_queries, key_heads, preferred_element_type=jnp.float32
    ) * (1.0 / math.sqrt(HEAD_SIZE))
    seen = (start_pos + lax.iota(jnp.int32, length))[None, :] < pos_rows[:, None]
    seen = seen[:, None, None, :]
    block_max = jnp.max(jnp.where(seen, scores, lowest), axis=-1)
    weights = jnp.where(seen, jnp.exp(scores - block_max[..., None]), 0.0)
    block_total = jnp.sum(weights, axis=-1)
    block_out = jnp.einsum(
        "tkgc,ckd->tkgd",
        weights.astype(jnp.bfloat16),
        value_heads,
        preferred_element_type=jnp.float32,
    )
    return (block_max, block_total, block_out)


def per_device(queries, trace_cache_keys, trace_cache_values, out_weight, positions, partner):
    length = trace_cache_keys.shape[0]
    tok_rows = queries.shape[0]
    local_kv = trace_cache_keys.shape[1] // HEAD_SIZE
    query_group = QUERY_HEADS // KEY_VALUE_HEADS
    start_pos = lax.axis_index("seq") * length
    every_pos = lax.all_gather(positions, "seq", axis=0, tiled=True)
    total_rows = every_pos.shape[0]
    piece = lax.all_gather(queries, "seq", axis=0, tiled=True)
    rows = piece.shape[0]
    width = math.gcd(rows, 64)
    stacked = (
        piece.reshape(rows // width, width, piece.shape[1]),
        every_pos.reshape(rows // width, width),
    )

    def single(inputs):
        return block_partials(inputs[0], trace_cache_keys, trace_cache_values, inputs[1], start_pos)

    maxima, totals, outputs = lax.map(single, stacked)
    maxima, totals, outputs = (
        maxima.reshape(rows, local_kv, query_group),
        totals.reshape(rows, local_kv, query_group),
        outputs.reshape(rows, local_kv, query_group, HEAD_SIZE),
    )
    highest = lax.pmax(maxima, "seq")
    factor = jnp.exp(maxima - highest)
    scaled_out = outputs * factor[..., None]
    scaled_total = totals * factor
    numerator, denominator = (
        lax.psum_scatter(scaled_out, "seq", scatter_dimension=0, tiled=True),
        lax.psum_scatter(scaled_total, "seq", scatter_dimension=0, tiled=True),
    )
    attended = (numerator / denominator[..., None]).astype(jnp.bfloat16).reshape(tok_rows, -1)
    terms = jnp.dot(
        lax.all_gather(attended, "seq", axis=0, tiled=True),
        out_weight,
        preferred_element_type=jnp.float32,
    )
    share = total_rows // lax.axis_size("kvh")
    first_row = lax.axis_index("kvh") * share
    mixed = lax.psum_scatter(terms, "kvh", scatter_dimension=0, tiled=True).astype(jnp.bfloat16)
    mixed_all = lax.all_gather(mixed, "kvh", axis=0, tiled=True)
    partner_rows = lax.dynamic_slice_in_dim(partner, first_row, share)
    paired = jnp.take(mixed_all, partner_rows, axis=0)
    contrast = (mixed.astype(jnp.float32) - paired.astype(jnp.float32)).astype(jnp.bfloat16)
    return (mixed, contrast)


def solution(mesh):
    placed = (P("seq", "kvh"), P("seq", "kvh"), P("seq", "kvh"), P("kvh", "seq"), P("seq"), P())
    return jax.shard_map(
        per_device,
        mesh=mesh,
        in_specs=placed,
        out_specs=(P("kvh", "seq"), P("kvh", "seq")),
        check_vma=False,
    )
```

profile of v0, /device:TPU:1, one launch (start us, length us, event | category | flops | bytes accessed | tf_op | source)
XLA Modules:
  0.0 868.9 jit_solution(10756353073167139028)
XLA Ops:
  10.8 20.0 %all-reduce = s32[512]{0:T(512)S(1)} all-reduce(s32[512]{0:T(512)S(1)} %dynamic-update-slice), channel_id=1, replica_groups=mesh['seq'=32,'kvh'=8] {'seq'}, use_global_device_ids=true, to_apply=%add | all-reduce | flops 512 | bytes 4096
  30.9 55.3 %all-gather.3.cloned.1.call-done = bf16[512,1024]{1,0:T(8,128)(2,1)} async-done(((bf16[16,1024]{1,0:T(8,128)(2,1)}), bf16[512,1024]{1,0:T(8,128)(2,1)}) %all-gather.3.cloned.1.call-update) | async-done | bytes 1048592 | tf_op jit(solution)/shard_map/all_gather | solution.py:49
  86.2 76.0 %while.14 = (s32[]{:T(128)}, f32[8,64,1,8]{3,1,2,0:T(8,128)S(1)}, f32[8,64,1,8]{3,1,2,0:T(8,128)S(1)}, f32[8,64,1,8,128]{4,3,1,2,0:T(8,128)S(1)}, s32[]{:T(128)}...) while((s32[]{:T(128)}, f32[8,64,1,8]{3,1,2,0:T(8,128)S(1)}, ...), condition=%wide.region_3.4_spmd, body=%wide.region_0.3_spmd.sunk | while | flops 1097075712 | bytes 33627028 | solution.py:60
  87.4 3.5 fusion.38
  93.1 2.6 fusion.39
  96.9 3.5 fusion.38
  102.6 2.6 fusion.39
  106.4 3.5 fusion.38
  112.1 2.6 fusion.39
  115.9 3.5 fusion.38
  121.6 2.6 fusion.39
  125.4 3.5 fusion.38
  131.1 2.6 fusion.39
  134.9 3.5 fusion.38
  140.6 2.6 fusion.39
  144.5 3.5 fusion.38
  150.1 2.6 fusion.39
  154.0 3.5 fusion.38
  162.3 112.5 %pmax.7 = f32[512,1,8]{0,2,1:T(8,128)S(1)} all-reduce(f32[512,1,8]{0,2,1:T(8,128)S(1)} %copy.17), channel_id=1, replica_groups=mesh['seq'=32,'kvh'=8] {'seq'}, use_global_device_ids=true, to_apply=%region_4.5 | all-reduce | flops 4096 | bytes 32768 | tf_op jit(solution)/shard_map/pmax | solution.py:66
  278.0 232.4 %reduce-scatter.10.cloned.1.call-done = f32[16,8]{1,0:T(8,128)} async-done(((f32[512,8]{1,0:T(8,128)}), f32[16,8]{1,0:T(8,128)}) %reduce-scatter.10.cloned.1.call-update) | async-done | bytes 528 | tf_op jit(solution)/shard_map/div | solution.py:74
  510.4 219.3 %reduce-scatter.6.cloned.1.call-done = f32[16,1,8,128]{3,2,0,1:T(8,128)} async-done(((f32[512,1,8,128]{3,2,0,1:T(8,128)}), f32[16,1,8,128]{3,2,0,1:T(8,128)}) %reduce-scatter.6.cloned.1.call-update) | async-done | bytes 65552 | tf_op jit(solution)/shard_map/reduce_scatter | solution.py:71
  731.3 76.4 %all-gather.5.cloned.1.call-done = bf16[512,1024]{1,0:T(8,128)(2,1)} async-done(((bf16[16,1024]{1,0:T(8,128)(2,1)}), bf16[512,1024]{1,0:T(8,128)(2,1)}) %all-gather.5.cloned.1.call-update) | async-done | bytes 1048592 | tf_op jit(solution)/shard_map/all_gather | solution.py:76
  811.0 32.6 %reduce-scatter.8.cloned.1.call-done = f32[64,256]{1,0:T(8,128)} async-done(((f32[512,256]{1,0:T(8,128)}), f32[64,256]{1,0:T(8,128)}) %reduce-scatter.8.cloned.1.call-update) | async-done | bytes 65552 | tf_op jit(solution)/shard_map/reduce_scatter | solution.py:82
  844.5 15.7 %all_gather.15 = bf16[512,256]{1,0:T(8,128)(2,1)S(1)} all-gather(bf16[64,256]{1,0:T(8,128)(2,1)S(1)} %convert_element_type.19), channel_id=1, replica_groups=mesh['seq'=32,'kvh'=8] {'kvh'}, dimensions={0}, use_global_device_ids=true | all-gather | bytes 294912 | tf_op jit(solution)/shard_map/all_gather | solution.py:83
  (108 shorter events, 43.9 us)
Async XLA Ops:
  7.2 800.6 %copy-start = (bf16[1024,256]{1,0:T(8,128)(2,1)S(1)}, bf16[1024,256]{1,0:T(8,128)(2,1)}, u32[]{:S(2)}) copy-start(bf16[1024,256]{1,0:T(8,128)(2,1)} %param.11) | copy-start | bytes 1572868
  7.2 79.0 %all-gather.3.cloned.1.call-start = ((), (), s32[]{:S(2)}) async-start(), calls=%async_computation.3 | async-start | bytes 1081344 | tf_op jit(solution)/shard_map/all_gather | solution.py:49
  7.9 502.5 %reduce-scatter.10.cloned.1.call-start = ((), (), s32[]{:S(2)}) async-start(), calls=%async_computation.7 | async-start | bytes 270336 | tf_op jit(solution)/shard_map/div | solution.py:74
  86.2 4.7 copy-start.2
  95.7 4.7 copy-start.2
  105.2 4.7 copy-start.2
  114.7 4.7 copy-start.2
  124.2 4.7 copy-start.2
  133.7 4.7 copy-start.2
  143.2 4.7 copy-start.2
  152.7 4.7 copy-start.2
  275.9 453.8 %reduce-scatter.6.cloned.1.call-start = ((), (), s32[]{:S(2)}) async-start(), calls=%async_computation.4 | async-start | bytes 2162688 | tf_op jit(solution)/shard_map/reduce_scatter | solution.py:71
  277.9 529.8 %all-gather.5.cloned.1.call-start = ((), (), s32[]{:S(2)}) async-start(), calls=%async_computation.5 | async-start | bytes 1081344 | tf_op jit(solution)/shard_map/all_gather | solution.py:76
  731.3 112.3 %reduce-scatter.8.cloned.1.call-start = ((), (), s32[]{:S(2)}) async-start(), calls=%async_computation.6 | async-start | bytes 589824 | tf_op jit(solution)/shard_map/reduce_scatter | solution.py:82
  844.5 17.9 %copy-start.1 = (bf16[64,256]{1,0:T(8,128)(2,1)}, bf16[64,256]{1,0:T(8,128)(2,1)S(1)}, u32[]{:S(2)}) copy-start(bf16[64,256]{1,0:T(8,128)(2,1)S(1)} %convert_element_type.19) | copy-start | bytes 98308
Sparse Core Ops, SparseCore 0:
  10.6 75.4 all-gather.2
  276.0 234.3 reduce-scatter.9
  514.7 214.9 reduce-scatter.5
  732.7 75.0 all-gather.4
  810.4 33.1 reduce-scatter.7
where the time goes:
time: 870 us; the launch traced here: 869 us
  waiting for transfers between devices  617 us (71%)
  blocking collectives  148 us (17%)
  matrix products  47.6 us (5%)
  other arithmetic  28.2 us (3%)
  between operations  14.5 us (2%)
  local copies, waits for them, and re-layouts  12.9 us (1%)
    div x1, waiting for transfers between devices, per_device(): numerator / denominator[..., None]  232 us
    reduce_scatter x1, waiting for transfers between devices, per_device(): lax.psum_scatter(scaled_out, 'seq', scatter_dimension=0, tiled=True)  219 us
    pmax x1, blocking collectives, per_device(): highest = lax.pmax(maxima, 'seq')  112 us
    all_gather x1, waiting for transfers between devices, per_device(): lax.all_gather(attended, 'seq', axis=0, tiled=True)  76.4 us
    all_gather x1, waiting for transfers between devices, per_device(): piece = lax.all_gather(queries, 'seq', axis=0, tiled=True)  55.3 us
    reduce_scatter x1, waiting for transfers between devices, per_device(): lax.psum_scatter(terms, 'kvh', scatter_dimension=0, tiled=True)  32.6 us
    dot_general x8, matrix products, block_partials(): jnp.einsum('tkgd,ckd->tkgc', grouped_queries, key_heads, preferred_elemen...  27.7 us
    reduce_sum x8, other arithmetic, block_partials(): block_total = jnp.sum(weights, axis=-1)  20.5 us
  transfers between devices with their start and end apart: 5, of which 5 were waited for; matrix products, arithmetic and copies ran while one was open for 1% of the time, Pallas kernels for 0%

commit v1 on v0

v1 whole, which is shorter than its diff:
```python
import math

import jax
import jax.numpy as jnp
from jax import lax
from jax.experimental import pallas as pl
from jax.experimental.pallas import tpu as pltpu
from jax.sharding import PartitionSpec as P

MESH = pl.DeviceIdType.MESH

HEADS = 8
HEAD = 128
NX, NZ, NK = 4, 8, 8
LENGTH = 4096
TOK = 16
CHUNK = NZ * TOK
TOKENS = NX * CHUNK
COLS = HEADS * HEAD
WIDE = COLS + 128
OUT = 256
SHARE = TOKENS // NK

GROUP = 4
ROWS = GROUP * CHUNK
STEP = 1024

LOW = -1e30
SCALE2 = math.log2(math.e) / math.sqrt(HEAD)


def dot(a, b):
    return lax.dot_general(a, b, (((1,), (0,)), ((), ())), preferred_element_type=jnp.float32)


def spread(t):
    lane = lax.broadcasted_iota(jnp.int32, t.shape, 1)
    t = jnp.where(lane < 8, t, 0.0)
    t = t + pltpu.roll(t, 8, 1) + pltpu.roll(t, 16, 1)
    first = t.astype(jnp.bfloat16).astype(jnp.float32)
    rest = t - first
    second = rest.astype(jnp.bfloat16).astype(jnp.float32)
    third = rest - second
    return jnp.where(lane < 8, first, jnp.where(lane < 16, second, third)).astype(jnp.bfloat16)


def gathered(t):
    t = t.astype(jnp.float32)
    return t + pltpu.roll(t, 120, 1) + pltpu.roll(t, 112, 1)


def merge(tiles, outs):
    logs = [gathered(t) for t in tiles]
    top = logs[0]
    for u in logs[1:]:
        top = jnp.maximum(top, u)
    shares = [jnp.exp2(u - top) for u in logs]
    total = shares[0]
    for w in shares[1:]:
        total = total + w
    inverse = 1.0 / total
    shares = [w * inverse for w in shares]
    merged = []
    for h in range(HEADS):
        acc = None
        for w, o in zip(shares, outs):
            term = w[:, h : h + 1] * o(h).astype(jnp.float32)
            acc = term if acc is None else acc + term
        merged.append(acc.astype(jnp.bfloat16))
    return merged, top + jnp.log2(total)


def kernel(
    q_ref, k_ref, v_ref, w_ref, pos_ref, partner_ref, mixed_ref, contrast_ref,
    k_buf, v_buf, w_buf, kt, vp, s0, s1, run, q_all, part, part_in, lse, zpart, z_in, att, pairs, terms, t_in,
    local_sem, qz_send, qz_recv, qx_send, qx_recv, px_send, px_recv, pz_send, pz_recv,
    az_send, az_recv, ax_send, ax_recv, t_send, t_recv,
):
    seq = lax.axis_index("seq")
    kvh = lax.axis_index("kvh")
    x = seq // NZ
    z = seq % NZ

    def x_peer(d):
        return (((x + d) % NX) * NZ + z, kvh)

    def z_peer(d):
        return (x * NZ + (z + d) % NZ, kvh)

    def k_peer(d):
        return (seq, (kvh + d) % NK)

    def block(i):
        return pl.ds(pl.multiple_of(i * TOK, TOK), TOK)

    loads = [
        pltpu.make_async_copy(src, dst, local_sem.at[i])
        for i, (src, dst) in enumerate(((k_ref, k_buf), (v_ref, v_buf), (w_ref, w_buf)))
    ]
    for c in loads:
        c.start()

    barrier = pltpu.get_barrier_semaphore()
    for d in range(1, NX):
        pl.semaphore_signal(barrier, inc=1, device_id=x_peer(d), device_id_type=MESH)
    for d in range(1, NZ):
        pl.semaphore_signal(barrier, inc=1, device_id=z_peer(d), device_id_type=MESH)
    for d in range(1, NK):
        pl.semaphore_signal(barrier, inc=1, device_id=k_peer(d), device_id_type=MESH)

    row = lax.broadcasted_iota(jnp.int32, (TOK, 128), 0)
    lane = lax.broadcasted_iota(jnp.int32, (TOK, 128), 1)
    counts = jnp.zeros((TOK, 128), jnp.int32)
    for i in range(TOK):
        counts = jnp.where(row == i, pos_ref[i], counts)
    high = lax.shift_right_logical(counts, 12)
    middle = lax.bitwise_and(lax.shift_right_logical(counts, 4), 255)
    low = lax.bitwise_and(counts, 15)
    counts = jnp.where(lane == 0, high, jnp.where(lane == 1, middle, low))
    q_all[x, block(z), 0:COLS] = q_ref[...]
    q_all[x, block(z), COLS:WIDE] = counts.astype(jnp.float32).astype(jnp.bfloat16)

    pl.semaphore_wait(barrier, NX + NZ + NK - 3)

    def qz(d):
        return pltpu.make_async_remote_copy(
            src_ref=q_all.at[x, block(z)], dst_ref=q_all.at[x, block(z)],
            send_sem=qz_send.at[d - 1], recv_sem=qz_recv.at[d - 1], device_id=z_peer(d), device_id_type=MESH)

    def qx(d):
        return pltpu.make_async_remote_copy(
            src_ref=q_all.at[x], dst_ref=q_all.at[x],
            send_sem=qx_send.at[d - 1], recv_sem=qx_recv.at[d - 1], device_id=x_peer(d), device_id_type=MESH)

    def px(d, half):
        owner = (x + d) % NX
        cols = pl.ds(0, 512) if half == 0 else pl.ds(512, WIDE - 512)
        return pltpu.make_async_remote_copy(
            src_ref=part.at[owner, :, cols], dst_ref=part_in.at[d - 1, :, cols],
            send_sem=px_send.at[half, d - 1], recv_sem=px_recv.at[half, d - 1], device_id=x_peer(d), device_id_type=MESH)

    def pz(d):
        return pltpu.make_async_remote_copy(
            src_ref=zpart.at[block((z + d) % NZ)], dst_ref=z_in.at[d - 1],
            send_sem=pz_send.at[d - 1], recv_sem=pz_recv.at[d - 1], device_id=z_peer(d), device_id_type=MESH)

    def az(d):
        return pltpu.make_async_remote_copy(
            src_ref=att.at[x, block(z)], dst_ref=att.at[x, block(z)],
            send_sem=az_send.at[d - 1], recv_sem=az_recv.at[d - 1], device_id=z_peer(d), device_id_type=MESH)

    def ax(d):
        return pltpu.make_async_remote_copy(
            src_ref=att.at[x], dst_ref=att.at[x],
            send_sem=ax_send.at[d - 1], recv_sem=ax_recv.at[d - 1], device_id=x_peer(d), device_id_type=MESH)

    def tk(d):
        rows = pl.ds(pl.multiple_of(((kvh + d) % NK) * SHARE, SHARE), SHARE)
        return pltpu.make_async_remote_copy(
            src_ref=terms.at[rows], dst_ref=t_in.at[kvh],
            send_sem=t_send.at[d - 1], recv_sem=t_recv.at[d - 1], device_id=k_peer(d), device_id_type=MESH)

    for d in range(1, NZ):
        qz(d).start()

    loads[0].wait()
    kt[...] = k_buf[...].T
    loads[1].wait()
    vp[:, 0:HEAD] = v_buf[...]
    vp[:, HEAD:] = jnp.where(lax.broadcasted_iota(jnp.int32, (LENGTH, 128), 1) == 0, 1.0, 0.0).astype(jnp.bfloat16)
    pairs[...] = jnp.where(
        lax.broadcasted_iota(jnp.int32, (TOKENS, TOKENS), 0) == partner_ref[...], 1.0, 0.0).astype(jnp.bfloat16)
    loads[2].wait()

    for d in range(1, NZ):
        qz(d).wait_recv()
    for d in range(1, NX):
        qx(d).start()

    start = seq * LENGTH
    run_of = (run.at[0], run.at[1])

    def offset(p):
        return p + p // 2 - 2 * (p // 3)

    def attention(a_chunk, a_half, b_chunk, b_half):
        if a_chunk is not None:
            a_x = (x + offset(a_chunk)) % NX
            q = jnp.concatenate(
                [q_all[a_x, :, (a_half * GROUP + j) * HEAD : (a_half * GROUP + j + 1) * HEAD] for j in range(GROUP)], axis=0)
            c = q_all[a_x, :, COLS:WIDE].astype(jnp.float32)
            count = (c[:, 0:1] * 4096.0 + c[:, 1:2] * 16.0 + c[:, 2:3]).astype(jnp.int32) - start
            a_s = (s0, s1)[a_half]
            a_run = None
        if b_chunk is not None:
            b_s = (s0, s1)[b_half]
            top = jnp.maximum(jnp.max(run_of[b_half][...], axis=1, keepdims=True), -1e29)
            total = None
        for i in range(LENGTH // STEP):
            cols = pl.ds(i * STEP, STEP)
            if a_chunk is not None:
                s = dot(q, kt[:, cols]) * SCALE2
                seen = (i * STEP + lax.broadcasted_iota(jnp.int32, (CHUNK, STEP), 1)) < count
                s = jnp.where(seen[None], s.reshape(GROUP, CHUNK, STEP), LOW).reshape(ROWS, STEP)
                a_s[:, cols] = s
                for j in range(STEP // 128):
                    m = s[:, j * 128 : (j + 1) * 128]
                    a_run = m if a_run is None else jnp.maximum(a_run, m)
            if b_chunk is not None:
                o = dot(jnp.exp2(b_s[:, cols] - top).astype(jnp.bfloat16), vp[cols, :])
                total = o if total is None else total + o
        if a_chunk is not None:
            run_of[a_half][...] = a_run
        if b_chunk is not None:
            b_x = (x + offset(b_chunk)) % NX
            weight = total[:, HEAD : HEAD + 1]
            some = weight > 0.0
            weight = jnp.where(some, weight, 1.0)
            out = total[:, 0:HEAD] / weight
            log = jnp.where(some, top + jnp.log2(weight), LOW)
            lanes = lax.broadcasted_iota(jnp.int32, (CHUNK, 128), 1)
            tile = jnp.zeros((CHUNK, 128), jnp.float32) if b_half == 0 else lse[...]
            for j in range(GROUP):
                h = b_half * GROUP + j
                part[b_x, :, h * HEAD : (h + 1) * HEAD] = out[j * CHUNK : (j + 1) * CHUNK].astype(jnp.bfloat16)
                tile = jnp.where(lanes == h, log[j * CHUNK : (j + 1) * CHUNK], tile)
            if b_half == 0:
                lse[...] = tile
            else:
                part[b_x, :, COLS:WIDE] = spread(tile)

    attention(0, 0, None, None)

    def pair(p, _):
        attention(p, 1, p, 0)

        @pl.when(p > 0)
        def _():
            px(offset(p), 0).start()

        qx(NX - offset(p + 1)).wait_recv()
        attention(p + 1, 0, p, 1)

        @pl.when(p > 0)
        def _():
            px(offset(p), 1).start()

        return 0

    lax.fori_loop(0, NX - 1, pair, 0)
    attention(NX - 1, 1, NX - 1, 0)
    px(2, 0).start()
    attention(None, None, NX - 1, 1)
    px(2, 1).start()

    for d in (1, 3, 2):
        px(d, 0).wait_recv()
        px(d, 1).wait_recv()
    own = lambda h: part[x, :, h * HEAD : (h + 1) * HEAD]
    others = [lambda h, d=d: part_in[d, :, h * HEAD : (h + 1) * HEAD] for d in range(NX - 1)]
    merged, log = merge([part[x, :, COLS:WIDE]] + [part_in[d, :, COLS:WIDE] for d in range(NX - 1)], [own] + others)
    for h in range(HEADS):
        zpart[:, h * HEAD : (h + 1) * HEAD] = merged[h]
    zpart[:, COLS:WIDE] = spread(log)
    for d in range(1, NZ):
        pz(d).start()

    for d in range(1, NZ):
        pz(d).wait_recv()
    own = lambda h: zpart[block(z), h * HEAD : (h + 1) * HEAD]
    others = [lambda h, d=d: z_in[d, :, h * HEAD : (h + 1) * HEAD] for d in range(NZ - 1)]
    merged, _ = merge([zpart[block(z), COLS:WIDE]] + [z_in[d, :, COLS:WIDE] for d in range(NZ - 1)], [own] + others)
    for h in range(HEADS):
        att[x, block(z), h * HEAD : (h + 1) * HEAD] = merged[h]

    for d in range(1, NZ):
        az(d).start()
    for d in range(1, NZ):
        az(d).wait_recv()
    for d in range(1, NX):
        ax(d).start()

    def project(source):
        rows = pl.ds(pl.multiple_of(source * CHUNK, CHUNK), CHUNK)
        terms[rows, 0:OUT] = dot(att[source], w_buf[...]).astype(jnp.bfloat16)

    project(x)
    for d in (1, 3, 2):
        ax(d).wait_recv()
        project((x + NX - d) % NX)

    terms[:, OUT:] = dot(pairs[...], terms[:, 0:OUT]).astype(jnp.bfloat16)
    for d in range(1, NK):
        tk(d).start()
    t_in[kvh] = terms[pl.ds(pl.multiple_of(kvh * SHARE, SHARE), SHARE)]
    for d in range(1, NK):
        tk(d).wait_recv()
    total = t_in[0].astype(jnp.float32)
    for i in range(1, NK):
        total = total + t_in[i].astype(jnp.float32)
    total = total.astype(jnp.bfloat16)
    mixed_ref[...] = total[:, 0:OUT]
    contrast_ref[...] = (total[:, 0:OUT].astype(jnp.float32) - total[:, OUT:].astype(jnp.float32)).astype(jnp.bfloat16)

    for d in range(1, NX):
        qx(d).wait_send()
        px(d, 0).wait_send()
        px(d, 1).wait_send()
        ax(d).wait_send()
    for d in range(1, NZ):
        qz(d).wait_send()
        pz(d).wait_send()
        az(d).wait_send()
    for d in range(1, NK):
        tk(d).wait_send()


def per_device(queries, keys, values, out_weight, positions, partner):
    bf, f32 = jnp.bfloat16, jnp.float32
    vmem = pl.BlockSpec(memory_space=pltpu.VMEM)
    any_ = pl.BlockSpec(memory_space=pl.ANY)
    dma = pltpu.SemaphoreType.DMA
    return pl.pallas_call(
        kernel,
        out_shape=(jax.ShapeDtypeStruct((SHARE, OUT), bf),) * 2,
        in_specs=[vmem, any_, any_, any_, pl.BlockSpec(memory_space=pltpu.SMEM), vmem],
        out_specs=(vmem, vmem),
        scratch_shapes=[
            pltpu.VMEM((LENGTH, HEAD), bf),
            pltpu.VMEM((LENGTH, HEAD), bf),
            pltpu.VMEM((COLS, OUT), bf),
            pltpu.VMEM((HEAD, LENGTH), bf),
            pltpu.VMEM((LENGTH, 2 * HEAD), bf),
            pltpu.VMEM((ROWS, LENGTH), f32),
            pltpu.VMEM((ROWS, LENGTH), f32),
            pltpu.VMEM((2, ROWS, 128), f32),
            pltpu.VMEM((NX, CHUNK, WIDE), bf),
            pltpu.VMEM((NX, CHUNK, WIDE), bf),
            pltpu.VMEM((NX - 1, CHUNK, WIDE), bf),
            pltpu.VMEM((CHUNK, 128), f32),
            pltpu.VMEM((CHUNK, WIDE), bf),
            pltpu.VMEM((NZ - 1, TOK, WIDE), bf),
            pltpu.VMEM((NX, CHUNK, COLS), bf),
            pltpu.VMEM((TOKENS, TOKENS), bf),
            pltpu.VMEM((TOKENS, 2 * OUT), bf),
            pltpu.VMEM((NK, SHARE, 2 * OUT), bf),
            dma((3,)),
            dma((NZ - 1,)), dma((NZ - 1,)),
            dma((NX - 1,)), dma((NX - 1,)),
            dma((2, NX - 1)), dma((2, NX - 1)),
            dma((NZ - 1,)), dma((NZ - 1,)),
            dma((NZ - 1,)), dma((NZ - 1,)),
            dma((NX - 1,)), dma((NX - 1,)),
            dma((NK - 1,)), dma((NK - 1,)),
        ],
        compiler_params=pltpu.CompilerParams(
            collective_id=0, has_side_effects=True, vmem_limit_bytes=56 * 2**20),
    )(queries, keys, values, out_weight, positions, partner.reshape(1, TOKENS))


def solution(mesh):
    placed = (P("seq", "kvh"), P("seq", "kvh"), P("seq", "kvh"), P("kvh", "seq"), P("seq"), P())
    return jax.shard_map(
        per_device,
        mesh=mesh,
        in_specs=placed,
        out_specs=(P("kvh", "seq"), P("kvh", "seq")),
        check_vma=False,
    )
```

time: 870 us -> 101 us (0.12)
  waiting for transfers between devices: 617 us -> 0 us
  blocking collectives: 148 us -> 0 us
  Pallas kernels: 0 us -> 96.3 us
  matrix products: 47.6 us -> 0 us
  other arithmetic: 28.2 us -> 0 us
  between operations: 14.5 us -> 0.65 us
  local copies, waits for them, and re-layouts: 12.9 us -> 2 us
    reduce_scatter x2 -> x0, waiting for transfers between devices: 252 us -> none  [the longest x1 219 us: per_device(): lax.psum_scatter(scaled_out, 'seq', scatter_dimension=0, tiled=True)]
    div x1 -> x0, waiting for transfers between devices: 232 us -> none  [per_device(): numerator / denominator[..., None]]
    all_gather x2 -> x0, waiting for transfers between devices: 132 us -> none  [the longest x1 76.4 us: per_device(): lax.all_gather(attended, 'seq', axis=0, tiled=True)]
    pmax x1 -> x0, blocking collectives: 112 us -> none  [per_device(): highest = lax.pmax(maxima, 'seq')]
    pallas_call x0 -> x1, Pallas kernels: none -> 96.3 us  [per_device(): pl.pallas_call(kernel, out_shape=(jax.ShapeDtypeStruct((SHARE, OUT), bf),...]
    dot_general x17 -> x0, matrix products: 47.6 us -> none  [the longest x8 27.7 us: block_partials(): jnp.einsum('tkgd,ckd->tkgc', grouped_queries, key_heads, preferred_elemen...]
    reduce_sum x8 -> x0, other arithmetic: 20.5 us -> none  [block_partials(): block_total = jnp.sum(weights, axis=-1)]
    unnamed x1 -> x0, blocking collectives: 20 us -> none
  transfers between devices with their start and end apart: 5 -> 0, of which waited for: 5 -> 0; matrix products, arithmetic and copies ran while one was open for 1% -> 0% of each run, Pallas kernels for 0% -> 0%
where the time goes in v1:
time: 101 us; the launch traced here: 98.9 us
  Pallas kernels  96.3 us (95%)
  local copies, waits for them, and re-layouts  2 us (2%)
    pallas_call x1, Pallas kernels, per_device(): pl.pallas_call(kernel, out_shape=(jax.ShapeDtypeStruct((SHARE, OUT), bf),...  96.3 us

profile of v1, /device:TPU:1, one launch (start us, length us, event | category | flops | bytes accessed | tf_op | source)
XLA Modules:
  0.0 98.9 jit_solution(16069978442956670541)
XLA Ops:
  0.6 96.3 %shard_map.77 = (bf16[64,256]{1,0:T(8,128)(2,1)}, bf16[64,256]{1,0:T(8,128)(2,1)}) custom-call(bf16[16,1024]{1,0:T(8,128)(2,1)} %q_ref.1, bf16[4096,128]{1,0:T(8,128)(2,1)} %k_ref.1, bf16[4096,128]{1,0:T(8,128)(2,1)} %v_ref.1, bf16[1024,256]{1,0:T(8,128)(2,1)} %w_ref.1, s32[16]{0:T(128)} %pos_ref.1, s32[1,512]{1,0:T(1,128)} %bitcast.1), custom_call_target="tpu_custom_call" | custom-call | tf_op jit(solution)/shard_map/pallas_call | solution.py:323
  96.9 0.0 copy-start
  96.9 1.4 %copy.10 = bf16[64,256]{1,0:T(8,128)(2,1)} copy(bf16[64,256]{1,0:T(8,128)(2,1)} %get-tuple-element.4) | data formatting | bytes 65536
  98.3 0.0 copy-done
  98.3 0.6 copy.11
Async XLA Ops:
  96.9 1.4 %copy-start = (bf16[64,256]{1,0:T(8,128)(2,1)S(1)}, bf16[64,256]{1,0:T(8,128)(2,1)}, u32[]{:S(2)}) copy-start(bf16[64,256]{1,0:T(8,128)(2,1)} %get-tuple-element.5) | copy-start | bytes 98308

commit v2 on v1

v2 whole, which is shorter than its diff:
```python
import math

import jax
import jax.numpy as jnp
from jax import lax
from jax.experimental import pallas as pl
from jax.experimental.pallas import tpu as pltpu
from jax.sharding import PartitionSpec as P

MESH = pl.DeviceIdType.MESH

HEADS = 8
HEAD = 128
NX, NZ, NK = 4, 8, 8
LENGTH = 4096
TOK = 16
CHUNK = NZ * TOK
TOKENS = NX * CHUNK
COLS = HEADS * HEAD
WIDE = COLS + 128
OUT = 256
SHARE = TOKENS // NK

SLAB = NX * TOK
ROWS = HEADS * SLAB
STEP = 1024

LOW = -1e30
SCALE2 = math.log2(math.e) / math.sqrt(HEAD)


def dot(a, b):
    return lax.dot_general(a, b, (((1,), (0,)), ((), ())), preferred_element_type=jnp.float32)


def spread(t):
    lane = lax.broadcasted_iota(jnp.int32, t.shape, 1)
    t = jnp.where(lane < 8, t, 0.0)
    t = t + pltpu.roll(t, 8, 1) + pltpu.roll(t, 16, 1)
    first = t.astype(jnp.bfloat16).astype(jnp.float32)
    rest = t - first
    second = rest.astype(jnp.bfloat16).astype(jnp.float32)
    third = rest - second
    return jnp.where(lane < 8, first, jnp.where(lane < 16, second, third)).astype(jnp.bfloat16)


def gathered(t):
    t = t.astype(jnp.float32)
    return t + pltpu.roll(t, 120, 1) + pltpu.roll(t, 112, 1)


def merge(tiles, outs):
    logs = [gathered(t) for t in tiles]
    top = logs[0]
    for u in logs[1:]:
        top = jnp.maximum(top, u)
    shares = [jnp.exp2(u - top) for u in logs]
    total = shares[0]
    for w in shares[1:]:
        total = total + w
    inverse = 1.0 / total
    shares = [w * inverse for w in shares]
    merged = []
    for h in range(HEADS):
        acc = None
        for w, o in zip(shares, outs):
            term = w[:, h : h + 1] * o(h).astype(jnp.float32)
            acc = term if acc is None else acc + term
        merged.append(acc.astype(jnp.bfloat16))
    return merged, top + jnp.log2(total)


def kernel(
    q_ref, k_ref, v_ref, w_ref, pos_ref, partner_ref, total_ref,
    k_buf, v_buf, w_buf, kt, vp, s0, s1, run, q_all, part, part_in, zpart, z_in, att, pairs, terms, t_out, t_in, p_out, p_in,
    local_sem, qx_send, qx_recv, up_send, up_recv, down_send, down_recv, px_send, px_recv, pz_send, pz_recv,
    az_send, az_recv, right_send, right_recv, left_send, left_recv, far_send, far_recv, t_send, t_recv, p_send, p_recv,
):
    seq = lax.axis_index("seq")
    kvh = lax.axis_index("kvh")
    x = seq // NZ
    z = seq % NZ

    def x_peer(d):
        return (((x + d) % NX) * NZ + z, kvh)

    def z_peer(d):
        return (x * NZ + (z + d) % NZ, kvh)

    def k_peer(d):
        return (seq, (kvh + d) % NK)

    def block(i):
        return pl.ds(pl.multiple_of(i * TOK, TOK), TOK)

    def remote(src, dst, send, recv, peer):
        return pltpu.make_async_remote_copy(
            src_ref=src, dst_ref=dst, send_sem=send, recv_sem=recv, device_id=peer, device_id_type=MESH)

    loads = [
        pltpu.make_async_copy(src, dst, local_sem.at[i])
        for i, (src, dst) in enumerate(((k_ref, k_buf), (v_ref, v_buf), (w_ref, w_buf)))
    ]
    for c in loads:
        c.start()

    barrier = pltpu.get_barrier_semaphore()
    for d in range(1, NX):
        pl.semaphore_signal(barrier, inc=1, device_id=x_peer(d), device_id_type=MESH)
    for d in range(1, NZ):
        pl.semaphore_signal(barrier, inc=1, device_id=z_peer(d), device_id_type=MESH)
    for d in range(1, NK):
        pl.semaphore_signal(barrier, inc=1, device_id=k_peer(d), device_id_type=MESH)

    row = lax.broadcasted_iota(jnp.int32, (TOK, 128), 0)
    lane = lax.broadcasted_iota(jnp.int32, (TOK, 128), 1)
    counts = jnp.zeros((TOK, 128), jnp.int32)
    for i in range(TOK):
        counts = jnp.where(row == i, pos_ref[i], counts)
    high = lax.shift_right_logical(counts, 12)
    middle = lax.bitwise_and(lax.shift_right_logical(counts, 4), 255)
    low = lax.bitwise_and(counts, 15)
    counts = jnp.where(lane == 0, high, jnp.where(lane == 1, middle, low))
    q_all[z, block(x), 0:COLS] = q_ref[...]
    q_all[z, block(x), COLS:WIDE] = counts.astype(jnp.float32).astype(jnp.bfloat16)

    pl.semaphore_wait(barrier, NX + NZ + NK - 3)

    def qx(d):
        here = q_all.at[z, block(x)]
        return remote(here, here, qx_send.at[d - 1], qx_recv.at[d - 1], x_peer(d))

    def up(k, last=False):
        slab = q_all.at[(z + NZ + 1 - k) % NZ]
        if last:
            slab = slab.at[pl.ds(0, SLAB // 2)]
        return remote(slab, slab, up_send.at[k - 1], up_recv.at[k - 1], z_peer(1))

    def down(k, last=False):
        slab = q_all.at[(z + k - 1) % NZ]
        if last:
            slab = slab.at[pl.ds(SLAB // 2, SLAB // 2)]
        return remote(slab, slab, down_send.at[k - 1], down_recv.at[k - 1], z_peer(NZ - 1))

    def px(n, d):
        return remote(part.at[n, block((x + d) % NX)], part_in.at[n, d - 1],
                      px_send.at[n, d - 1], px_recv.at[n, d - 1], x_peer(d))

    def offset(n):
        m = n + (n // 6) * (13 - 2 * n)
        return ((m + 1) // 2 * (2 * (m % 2) - 1) + NZ) % NZ

    def pz(n):
        return remote(zpart.at[n], z_in.at[n], pz_send.at[n - 1], pz_recv.at[n - 1], z_peer(offset(n)))

    def az(d):
        here = att.at[x, block(z)]
        return remote(here, here, az_send.at[d - 1], az_recv.at[d - 1], z_peer(d))

    def right(d):
        here = att.at[x, block((z + NZ - d) % NZ)]
        return remote(here, here, right_send.at[d], right_recv.at[d], x_peer(1))

    def left(d):
        here = att.at[x, block((z + NZ - d) % NZ)]
        return remote(here, here, left_send.at[d], left_recv.at[d], x_peer(NX - 1))

    def far(d):
        if d % 2 == 0:
            here = att.at[(x + NX - 1) % NX, block((z + NZ - d) % NZ)]
            return remote(here, here, far_send.at[d], far_recv.at[d], x_peer(1))
        here = att.at[(x + 1) % NX, block((z + NZ - d) % NZ)]
        return remote(here, here, far_send.at[d], far_recv.at[d], x_peer(NX - 1))

    def tk(d):
        return remote(t_out.at[(kvh + d) % NK], t_in.at[kvh], t_send.at[d - 1], t_recv.at[d - 1], k_peer(d))

    def pk(d):
        return remote(p_out.at[(kvh + d) % NK], p_in.at[kvh], p_send.at[d - 1], p_recv.at[d - 1], k_peer(d))

    for d in range(1, NX):
        qx(d).start()

    loads[0].wait()
    kt[...] = k_buf[...].T

    for d in range(1, NX):
        qx(d).wait_recv()
    up(1).start()
    down(1).start()

    start = seq * LENGTH
    run_of = (run.at[0], run.at[1])

    def attention(a, a_slot, b, b_slot):
        if a is not None:
            a_z = (z + offset(a)) % NZ
            q = jnp.concatenate([q_all[a_z, :, h * HEAD : (h + 1) * HEAD] for h in range(HEADS)], axis=0)
            c = q_all[a_z, :, COLS:WIDE].astype(jnp.float32)
            count = (c[:, 0:1] * 4096.0 + c[:, 1:2] * 16.0 + c[:, 2:3]).astype(jnp.int32) - start
            a_s = (s0, s1)[a_slot]
            a_run = None
        if b is not None:
            b_s = (s0, s1)[b_slot]
            top = jnp.maximum(jnp.max(run_of[b_slot][...], axis=1, keepdims=True), -1e29)
            total = None
        for i in range(LENGTH // STEP):
            cols = pl.ds(i * STEP, STEP)
            if a is not None:
                s = dot(q, kt[:, cols]) * SCALE2
                seen = (i * STEP + lax.broadcasted_iota(jnp.int32, (SLAB, STEP), 1)) < count
                s = jnp.where(seen[None], s.reshape(HEADS, SLAB, STEP), LOW).reshape(ROWS, STEP)
                a_s[:, cols] = s
                for j in range(STEP // 128):
                    m = s[:, j * 128 : (j + 1) * 128]
                    a_run = m if a_run is None else jnp.maximum(a_run, m)
            if b is not None:
                o = dot(jnp.exp2(b_s[:, cols] - top).astype(jnp.bfloat16), vp[cols, :])
                total = o if total is None else total + o
        if a is not None:
            run_of[a_slot][...] = a_run
        if b is not None:
            weight = total[:, HEAD : HEAD + 1]
            some = weight > 0.0
            weight = jnp.where(some, weight, 1.0)
            out = total[:, 0:HEAD] / weight
            log = jnp.where(some, top + jnp.log2(weight), LOW)
            lanes = lax.broadcasted_iota(jnp.int32, (SLAB, 128), 1)
            tile = jnp.zeros((SLAB, 128), jnp.float32)
            for h in range(HEADS):
                part[b, :, h * HEAD : (h + 1) * HEAD] = out[h * SLAB : (h + 1) * SLAB].astype(jnp.bfloat16)
                tile = jnp.where(lanes == h, log[h * SLAB : (h + 1) * SLAB], tile)
            part[b, :, COLS:WIDE] = spread(tile)
            for d in range(1, NX):
                px(b, d).start()

    def over_x(n):
        for d in range(1, NX):
            px(n, d).wait_recv()
        outs = [lambda h: part[n, block(x), h * HEAD : (h + 1) * HEAD]]
        outs += [lambda h, d=d: part_in[n, d, :, h * HEAD : (h + 1) * HEAD] for d in range(NX - 1)]
        tiles = [part[n, block(x), COLS:WIDE]] + [part_in[n, d, :, COLS:WIDE] for d in range(NX - 1)]
        merged, log = merge(tiles, outs)
        for h in range(HEADS):
            zpart[n, :, h * HEAD : (h + 1) * HEAD] = merged[h]
        zpart[n, :, COLS:WIDE] = spread(log)

    attention(0, 0, None, None)
    loads[1].wait()
    vp[:, 0:HEAD] = v_buf[...]
    vp[:, HEAD:] = jnp.where(lax.broadcasted_iota(jnp.int32, (LENGTH, 128), 1) == 0, 1.0, 0.0).astype(jnp.bfloat16)
    pairs[...] = jnp.where(
        lax.broadcasted_iota(jnp.int32, (TOKENS, TOKENS), 0) == partner_ref[...], 1.0, 0.0).astype(jnp.bfloat16)
    loads[2].wait()

    def two(j, _):
        up(j + 1).wait_recv()
        down(j + 1).wait_recv()

        @pl.when(j < 2)
        def _():
            up(j + 2).start()
            down(j + 2).start()

        @pl.when(j == 2)
        def _():
            up(4, True).start()
            down(4, True).start()

        attention(2 * j + 1, 1, 2 * j, 0)

        @pl.when(j > 0)
        def _():
            over_x(2 * j - 1)
            pz(2 * j - 1).start()

        @pl.when(j == 2)
        def _():
            up(4, True).wait_recv()
            down(4, True).wait_recv()

        attention(2 * j + 2, 0, 2 * j + 1, 1)
        over_x(2 * j)

        @pl.when(j > 0)
        def _():
            pz(2 * j).start()

        return 0

    lax.fori_loop(0, NZ // 2 - 1, two, 0)
    attention(NZ - 1, 1, NZ - 2, 0)
    over_x(NZ - 3)
    pz(NZ - 3).start()
    attention(None, None, NZ - 1, 1)
    over_x(NZ - 2)
    pz(NZ - 2).start()
    over_x(NZ - 1)
    pz(NZ - 1).start()

    for n in range(1, NZ):
        pz(n).wait_recv()
    outs = [lambda h: zpart[0, :, h * HEAD : (h + 1) * HEAD]]
    outs += [lambda h, n=n: z_in[n, :, h * HEAD : (h + 1) * HEAD] for n in range(1, NZ)]
    merged, _ = merge([zpart[0, :, COLS:WIDE]] + [z_in[n, :, COLS:WIDE] for n in range(1, NZ)], outs)
    for h in range(HEADS):
        att[x, block(z), h * HEAD : (h + 1) * HEAD] = merged[h]

    order = (0, 1, 7, 2, 6, 3, 5, 4)
    for d in order[1:]:
        az(d).start()

    def relay(d):
        (right if d % 2 == 0 else left)(d).wait_recv()
        far(d).start()

    for i, d in enumerate(order):
        if d > 0:
            az(d).wait_recv()
        right(d).start()
        left(d).start()
        if i >= 2:
            relay(order[i - 2])

    def project(source):
        rows = pl.ds(pl.multiple_of(source * CHUNK, CHUNK), CHUNK)
        t = dot(att[source], w_buf[...]).astype(jnp.bfloat16)
        terms[rows] = t
        for j in range(CHUNK // SHARE):
            owner = source * (CHUNK // SHARE) + j
            t_out[owner] = t[j * SHARE : (j + 1) * SHARE]

            @pl.when(owner != kvh)
            def _():
                tk((owner + NK - kvh) % NK).start()

    project(x)
    relay(order[6])
    relay(order[7])
    for d in order:
        (left if d % 2 == 0 else right)(d).wait_recv()
    project((x + 1) % NX)
    project((x + NX - 1) % NX)
    for d in order:
        far(d).wait_recv()
    project((x + 2) % NX)

    partners = dot(pairs[...], terms[...]).astype(jnp.bfloat16)
    for i in range(NK):
        p_out[i] = partners[i * SHARE : (i + 1) * SHARE]
    for d in range(1, NK):
        pk(d).start()
    t_in[kvh] = t_out[kvh]
    p_in[kvh] = p_out[kvh]

    def total(ref):
        t = ref[0].astype(jnp.float32)
        for i in range(1, NK):
            t = t + ref[i].astype(jnp.float32)
        return t.astype(jnp.bfloat16)

    for d in range(1, NK):
        tk(d).wait_recv()
    total_ref[:, 0:OUT] = total(t_in)
    for d in range(1, NK):
        pk(d).wait_recv()
    total_ref[:, OUT:] = total(p_in)

    for d in range(1, NX):
        qx(d).wait_send()
        for n in range(NZ):
            px(n, d).wait_send()
    for k in range(1, NZ // 2 + 1):
        up(k, k == NZ // 2).wait_send()
        down(k, k == NZ // 2).wait_send()
    for d in range(1, NZ):
        pz(d).wait_send()
        az(d).wait_send()
    for d in range(NZ):
        right(d).wait_send()
        left(d).wait_send()
        far(d).wait_send()
    for d in range(1, NK):
        tk(d).wait_send()
        pk(d).wait_send()


def per_device(queries, keys, values, out_weight, positions, partner):
    bf, f32 = jnp.bfloat16, jnp.float32
    vmem = pl.BlockSpec(memory_space=pltpu.VMEM)
    any_ = pl.BlockSpec(memory_space=pl.ANY)
    dma = pltpu.SemaphoreType.DMA
    total = pl.pallas_call(
        kernel,
        out_shape=jax.ShapeDtypeStruct((SHARE, 2 * OUT), bf),
        in_specs=[vmem, any_, any_, any_, pl.BlockSpec(memory_space=pltpu.SMEM), vmem],
        out_specs=vmem,
        scratch_shapes=[
            pltpu.VMEM((LENGTH, HEAD), bf),
            pltpu.VMEM((LENGTH, HEAD), bf),
            pltpu.VMEM((COLS, OUT), bf),
            pltpu.VMEM((HEAD, LENGTH), bf),
            pltpu.VMEM((LENGTH, 2 * HEAD), bf),
            pltpu.VMEM((ROWS, LENGTH), f32),
            pltpu.VMEM((ROWS, LENGTH), f32),
            pltpu.VMEM((2, ROWS, 128), f32),
            pltpu.VMEM((NZ, SLAB, WIDE), bf),
            pltpu.VMEM((NZ, SLAB, WIDE), bf),
            pltpu.VMEM((NZ, NX - 1, TOK, WIDE), bf),
            pltpu.VMEM((NZ, TOK, WIDE), bf),
            pltpu.VMEM((NZ, TOK, WIDE), bf),
            pltpu.VMEM((NX, CHUNK, COLS), bf),
            pltpu.VMEM((TOKENS, TOKENS), bf),
            pltpu.VMEM((TOKENS, OUT), bf),
            pltpu.VMEM((NK, SHARE, OUT), bf),
            pltpu.VMEM((NK, SHARE, OUT), bf),
            pltpu.VMEM((NK, SHARE, OUT), bf),
            pltpu.VMEM((NK, SHARE, OUT), bf),
            dma((3,)),
            dma((NX - 1,)), dma((NX - 1,)),
            dma((4,)), dma((4,)), dma((4,)), dma((4,)),
            dma((NZ, NX - 1)), dma((NZ, NX - 1)),
            dma((NZ - 1,)), dma((NZ - 1,)),
            dma((NZ - 1,)), dma((NZ - 1,)),
            dma((NZ,)), dma((NZ,)), dma((NZ,)), dma((NZ,)), dma((NZ,)), dma((NZ,)),
            dma((NK - 1,)), dma((NK - 1,)), dma((NK - 1,)), dma((NK - 1,)),
        ],
        compiler_params=pltpu.CompilerParams(
            collective_id=0, has_side_effects=True, vmem_limit_bytes=56 * 2**20),
    )(queries, keys, values, out_weight, positions, partner.reshape(1, TOKENS))
    mixed, other = total[:, 0:OUT], total[:, OUT:]
    return mixed, (mixed.astype(f32) - other.astype(f32)).astype(bf)


def solution(mesh):
    placed = (P("seq", "kvh"), P("seq", "kvh"), P("seq", "kvh"), P("kvh", "seq"), P("seq"), P())
    return jax.shard_map(
        per_device,
        mesh=mesh,
        in_specs=placed,
        out_specs=(P("kvh", "seq"), P("kvh", "seq")),
        check_vma=False,
    )
```

time: 101 us -> 85.4 us (0.85); the launches traced: 98.9 us -> 85.2 us
  Pallas kernels: 96.3 us -> 83.2 us
  local copies, waits for them, and re-layouts: 2 us -> 0 us
  other arithmetic: 0 us -> 1.41 us
    pallas_call x1, Pallas kernels: 96.3 us -> 83.2 us  [per_device(): pl.pallas_call(kernel, out_shape=jax.ShapeDtypeStruct((SHARE, 2 * OUT), b...]
    unnamed x4 -> x0, local copies, waits for them, and re-layouts: 2 us -> none
    convert_element_type x0 -> x1, other arithmetic: none -> 1.41 us  [per_device(): return (mixed, (mixed.astype(f32) - other.astype(f32)).astype(bf))]
where the time goes in v2:
time: 85.4 us; the launch traced here: 85.2 us
  Pallas kernels  83.2 us (97%)
  other arithmetic  1.41 us (2%)
    pallas_call x1, Pallas kernels, per_device(): pl.pallas_call(kernel, out_shape=jax.ShapeDtypeStruct((SHARE, 2 * OUT), b...  83.2 us

profile of v2, /device:TPU:1, one launch (start us, length us, event | category | flops | bytes accessed | tf_op | source)
XLA Modules:
  0.0 85.2 jit_solution(17069095655533679393)
XLA Ops:
  0.6 83.2 %shard_map.77 = bf16[64,512]{1,0:T(8,128)(2,1)} custom-call(bf16[16,1024]{1,0:T(8,128)(2,1)} %q_ref.1, bf16[4096,128]{1,0:T(8,128)(2,1)} %k_ref.1, bf16[4096,128]{1,0:T(8,128)(2,1)} %v_ref.1, bf16[1024,256]{1,0:T(8,128)(2,1)} %w_ref.1, s32[16]{0:T(128)} %pos_ref.1, s32[1,512]{1,0:T(1,128)} %bitcast.1), custom_call_target="tpu_custom_call" | custom-call | tf_op jit(solution)/shard_map/pallas_call | solution.py:393
  83.8 1.4 %subtract_convert_fusion = (bf16[64,256]{1,0:T(8,128)(2,1)}, bf16[64,256]{1,0:T(8,128)(2,1)}) fusion(bf16[64,512]{1,0:T(8,128)(2,1)} %shard_map.77), kind=kLoop, calls=%fused_computation | loop fusion | flops 65536 | bytes 131072 | tf_op jit(solution)/shard_map/convert_element_type | solution.py:432

commit v3 on v2

--- a/solution.py
+++ b/solution.py
@@ -31,6 +31,10 @@
 
 def dot(a, b):
     return lax.dot_general(a, b, (((1,), (0,)), ((), ())), preferred_element_type=jnp.float32)
+
+
+def dot_t(a, b):
+    return lax.dot_general(a, b, (((1,), (1,)), ((), ())), preferred_element_type=jnp.float32)
 
 
 def spread(t):
@@ -72,9 +76,9 @@
 
 def kernel(
     q_ref, k_ref, v_ref, w_ref, pos_ref, partner_ref, total_ref,
-    k_buf, v_buf, w_buf, kt, vp, s0, s1, run, q_all, part, part_in, zpart, z_in, att, pairs, terms, t_out, t_in, p_out, p_in,
-    local_sem, qx_send, qx_recv, up_send, up_recv, down_send, down_recv, px_send, px_recv, pz_send, pz_recv,
-    az_send, az_recv, right_send, right_recv, left_send, left_recv, far_send, far_recv, t_send, t_recv, p_send, p_recv,
+    k_buf, v_buf, w_buf, vp, s0, s1, run, q_all, part, part_in, zpart, z_in, att, pairs, terms, t_out, t_in, p_out, p_in,
+    local_sem, fq_send, fq_recv, up_send, up_recv, down_send, down_recv, px_send, px_recv, pz_send, pz_recv,
+    az_send, az_recv, ax_send, ax_recv, t_send, t_recv, p_send, p_recv,
 ):
     seq = lax.axis_index("seq")
     kvh = lax.axis_index("kvh")
@@ -107,7 +111,7 @@
     barrier = pltpu.get_barrier_semaphore()
     for d in range(1, NX):
         pl.semaphore_signal(barrier, inc=1, device_id=x_peer(d), device_id_type=MESH)
-    for d in range(1, NZ):
+    for d in (1, NZ - 1):
         pl.semaphore_signal(barrier, inc=1, device_id=z_peer(d), device_id_type=MESH)
     for d in range(1, NK):
         pl.semaphore_signal(barrier, inc=1, device_id=k_peer(d), device_id_type=MESH)
@@ -124,53 +128,48 @@
     q_all[z, block(x), 0:COLS] = q_ref[...]
     q_all[z, block(x), COLS:WIDE] = counts.astype(jnp.float32).astype(jnp.bfloat16)
 
-    pl.semaphore_wait(barrier, NX + NZ + NK - 3)
-
-    def qx(d):
-        here = q_all.at[z, block(x)]
-        return remote(here, here, qx_send.at[d - 1], qx_recv.at[d - 1], x_peer(d))
-
-    def up(k, last=False):
-        slab = q_all.at[(z + NZ + 1 - k) % NZ]
-        if last:
-            slab = slab.at[pl.ds(0, SLAB // 2)]
-        return remote(slab, slab, up_send.at[k - 1], up_recv.at[k - 1], z_peer(1))
-
-    def down(k, last=False):
-        slab = q_all.at[(z + k - 1) % NZ]
-        if last:
-            slab = slab.at[pl.ds(SLAB // 2, SLAB // 2)]
-        return remote(slab, slab, down_send.at[k - 1], down_recv.at[k - 1], z_peer(NZ - 1))
+    pl.semaphore_wait(barrier, NX + NK)
+
+    def up(k):
+        here = q_all.at[(z + NZ + 1 - k) % NZ, block(x)]
+        return remote(here, here, up_send.at[k - 1], up_recv.at[k - 1], z_peer(1))
+
+    def down(k):
+        here = q_all.at[(z + k - 1) % NZ, block(x)]
+        return remote(here, here, down_send.at[k - 1], down_recv.at[k - 1], z_peer(NZ - 1))
+
+    def fq(dz, e):
+        here = q_all.at[(z + dz) % NZ, block(x)]
+        return remote(here, here, fq_send.at[dz, e - 1], fq_recv.at[dz, e - 1], x_peer(e))
+
+    def hop(k):
+        up(k).wait_recv()
+        if k < NZ // 2:
+            down(k).wait_recv()
+            up(k + 1).start()
+        if k + 1 < NZ // 2:
+            down(k + 1).start()
+        for e in (1, 3, 2):
+            fq(NZ - k, e).start()
+            if k < NZ // 2:
+                fq(k, e).start()
 
     def px(n, d):
         return remote(part.at[n, block((x + d) % NX)], part_in.at[n, d - 1],
                       px_send.at[n, d - 1], px_recv.at[n, d - 1], x_peer(d))
 
-    def offset(n):
-        m = n + (n // 6) * (13 - 2 * n)
-        return ((m + 1) // 2 * (2 * (m % 2) - 1) + NZ) % NZ
+    order = (0, 1, 7, 2, 6, 3, 4, 5)
 
     def pz(n):
-        return remote(zpart.at[n], z_in.at[n], pz_send.at[n - 1], pz_recv.at[n - 1], z_peer(offset(n)))
+        return remote(zpart.at[n], z_in.at[n], pz_send.at[n - 1], pz_recv.at[n - 1], z_peer(order[n]))
 
     def az(d):
         here = att.at[x, block(z)]
         return remote(here, here, az_send.at[d - 1], az_recv.at[d - 1], z_peer(d))
 
-    def right(d):
+    def ax(d, e):
         here = att.at[x, block((z + NZ - d) % NZ)]
-        return remote(here, here, right_send.at[d], right_recv.at[d], x_peer(1))
-
-    def left(d):
-        here = att.at[x, block((z + NZ - d) % NZ)]
-        return remote(here, here, left_send.at[d], left_recv.at[d], x_peer(NX - 1))
-
-    def far(d):
-        if d % 2 == 0:
-            here = att.at[(x + NX - 1) % NX, block((z + NZ - d) % NZ)]
-            return remote(here, here, far_send.at[d], far_recv.at[d], x_peer(1))
-        here = att.at[(x + 1) % NX, block((z + NZ - d) % NZ)]
-        return remote(here, here, far_send.at[d], far_recv.at[d], x_peer(NX - 1))
+        return remote(here, here, ax_send.at[d, e - 1], ax_recv.at[d, e - 1], x_peer(e))
 
     def tk(d):
         return remote(t_out.at[(kvh + d) % NK], t_in.at[kvh], t_send.at[d - 1], t_recv.at[d - 1], k_peer(d))
@@ -178,23 +177,29 @@
     def pk(d):
         return remote(p_out.at[(kvh + d) % NK], p_in.at[kvh], p_send.at[d - 1], p_recv.at[d - 1], k_peer(d))
 
-    for d in range(1, NX):
-        qx(d).start()
-
-    loads[0].wait()
-    kt[...] = k_buf[...].T
-
-    for d in range(1, NX):
-        qx(d).wait_recv()
     up(1).start()
     down(1).start()
+    for e in (1, 3, 2):
+        fq(0, e).start()
+
+    loads[1].wait()
+    vp[:, 0:HEAD] = v_buf[...]
+    vp[:, HEAD:] = jnp.where(lax.broadcasted_iota(jnp.int32, (LENGTH, 128), 1) == 0, 1.0, 0.0).astype(jnp.bfloat16)
+    loads[0].wait()
 
     start = seq * LENGTH
     run_of = (run.at[0], run.at[1])
 
-    def attention(a, a_slot, b, b_slot):
+    def attention(a, a_slot, b, b_slot, done=None):
+        if done is not None:
+            for d in range(1, NX):
+                px(done, d).wait_recv()
         if a is not None:
-            a_z = (z + offset(a)) % NZ
+            for e in (1, 3, 2):
+                fq(order[a], e).wait_recv()
+            if a == 0:
+                hop(1)
+            a_z = (z + order[a]) % NZ
             q = jnp.concatenate([q_all[a_z, :, h * HEAD : (h + 1) * HEAD] for h in range(HEADS)], axis=0)
             c = q_all[a_z, :, COLS:WIDE].astype(jnp.float32)
             count = (c[:, 0:1] * 4096.0 + c[:, 1:2] * 16.0 + c[:, 2:3]).astype(jnp.int32) - start
@@ -207,7 +212,7 @@
         for i in range(LENGTH // STEP):
             cols = pl.ds(i * STEP, STEP)
             if a is not None:
-                s = dot(q, kt[:, cols]) * SCALE2
+                s = dot_t(q, k_buf[cols, :]) * SCALE2
                 seen = (i * STEP + lax.broadcasted_iota(jnp.int32, (SLAB, STEP), 1)) < count
                 s = jnp.where(seen[None], s.reshape(HEADS, SLAB, STEP), LOW).reshape(ROWS, STEP)
                 a_s[:, cols] = s
@@ -217,6 +222,8 @@
             if b is not None:
                 o = dot(jnp.exp2(b_s[:, cols] - top).astype(jnp.bfloat16), vp[cols, :])
                 total = o if total is None else total + o
+            if done is not None and i == 1:
+                over_x(done)
         if a is not None:
             run_of[a_slot][...] = a_run
         if b is not None:
@@ -233,10 +240,10 @@
             part[b, :, COLS:WIDE] = spread(tile)
             for d in range(1, NX):
                 px(b, d).start()
+        if done is not None and done > 0:
+            pz(done).start()
 
     def over_x(n):
-        for d in range(1, NX):
-            px(n, d).wait_recv()
         outs = [lambda h: part[n, block(x), h * HEAD : (h + 1) * HEAD]]
         outs += [lambda h, d=d: part_in[n, d, :, h * HEAD : (h + 1) * HEAD] for d in range(NX - 1)]
         tiles = [part[n, block(x), COLS:WIDE]] + [part_in[n, d, :, COLS:WIDE] for d in range(NX - 1)]
@@ -246,57 +253,27 @@
         zpart[n, :, COLS:WIDE] = spread(log)
 
     attention(0, 0, None, None)
-    loads[1].wait()
-    vp[:, 0:HEAD] = v_buf[...]
-    vp[:, HEAD:] = jnp.where(lax.broadcasted_iota(jnp.int32, (LENGTH, 128), 1) == 0, 1.0, 0.0).astype(jnp.bfloat16)
     pairs[...] = jnp.where(
         lax.broadcasted_iota(jnp.int32, (TOKENS, TOKENS), 0) == partner_ref[...], 1.0, 0.0).astype(jnp.bfloat16)
+    attention(None, None, 0, 0)
     loads[2].wait()
 
-    def two(j, _):
-        up(j + 1).wait_recv()
-        down(j + 1).wait_recv()
-
-        @pl.when(j < 2)
-        def _():
-            up(j + 2).start()
-            down(j + 2).start()
-
-        @pl.when(j == 2)
-        def _():
-            up(4, True).start()
-            down(4, True).start()
-
-        attention(2 * j + 1, 1, 2 * j, 0)
-
-        @pl.when(j > 0)
-        def _():
-            over_x(2 * j - 1)
-            pz(2 * j - 1).start()
-
-        @pl.when(j == 2)
-        def _():
-            up(4, True).wait_recv()
-            down(4, True).wait_recv()
-
-        attention(2 * j + 2, 0, 2 * j + 1, 1)
-        over_x(2 * j)
-
-        @pl.when(j > 0)
-        def _():
-            pz(2 * j).start()
-
-        return 0
-
-    lax.fori_loop(0, NZ // 2 - 1, two, 0)
-    attention(NZ - 1, 1, NZ - 2, 0)
-    over_x(NZ - 3)
-    pz(NZ - 3).start()
-    attention(None, None, NZ - 1, 1)
-    over_x(NZ - 2)
-    pz(NZ - 2).start()
-    over_x(NZ - 1)
-    pz(NZ - 1).start()
+    hop(2)
+    attention(1, 1, None, None)
+    attention(2, 0, 1, 1)
+    hop(3)
+    attention(3, 1, 2, 0, 0)
+    hop(4)
+    attention(4, 0, 3, 1, 1)
+    attention(5, 1, 4, 0, 2)
+    attention(6, 0, 5, 1, 3)
+    attention(7, 1, 6, 0, 4)
+    attention(None, None, 7, 1, 5)
+    for n in (NZ - 2, NZ - 1):
+        for d in range(1, NX):
+            px(n, d).wait_recv()
+        over_x(n)
+        pz(n).start()
 
     for n in range(1, NZ):
         pz(n).wait_recv()
@@ -306,21 +283,15 @@
     for h in range(HEADS):
         att[x, block(z), h * HEAD : (h + 1) * HEAD] = merged[h]
 
-    order = (0, 1, 7, 2, 6, 3, 5, 4)
-    for d in order[1:]:
+    near = (0, 1, 7, 2, 6, 3, 5, 4)
+    for e in (1, 3, 2):
+        ax(0, e).start()
+    for d in near[1:]:
         az(d).start()
-
-    def relay(d):
-        (right if d % 2 == 0 else left)(d).wait_recv()
-        far(d).start()
-
-    for i, d in enumerate(order):
-        if d > 0:
-            az(d).wait_recv()
-        right(d).start()
-        left(d).start()
-        if i >= 2:
-            relay(order[i - 2])
+    for d in near[1:]:
+        az(d).wait_recv()
+        for e in (1, 3, 2):
+            ax(d, e).start()
 
     def project(source):
         rows = pl.ds(pl.multiple_of(source * CHUNK, CHUNK), CHUNK)
@@ -335,15 +306,10 @@
                 tk((owner + NK - kvh) % NK).start()
 
     project(x)
-    relay(order[6])
-    relay(order[7])
-    for d in order:
-        (left if d % 2 == 0 else right)(d).wait_recv()
-    project((x + 1) % NX)
-    project((x + NX - 1) % NX)
-    for d in order:
-        far(d).wait_recv()
-    project((x + 2) % NX)
+    for e in (1, 3, 2):
+        for d in near:
+            ax(d, e).wait_recv()
+        project((x + NX - e) % NX)
 
     partners = dot(pairs[...], terms[...]).astype(jnp.bfloat16)
     for i in range(NK):
@@ -366,20 +332,18 @@
         pk(d).wait_recv()
     total_ref[:, OUT:] = total(p_in)
 
-    for d in range(1, NX):
-        qx(d).wait_send()
-        for n in range(NZ):
-            px(n, d).wait_send()
+    for n in range(NZ):
+        for e in range(1, NX):
+            fq(n, e).wait_send()
+            px(n, e).wait_send()
+            ax(n, e).wait_send()
     for k in range(1, NZ // 2 + 1):
-        up(k, k == NZ // 2).wait_send()
-        down(k, k == NZ // 2).wait_send()
+        up(k).wait_send()
+        if k < NZ // 2:
+            down(k).wait_send()
     for d in range(1, NZ):
         pz(d).wait_send()
         az(d).wait_send()
-    for d in range(NZ):
-        right(d).wait_send()
-        left(d).wait_send()
-        far(d).wait_send()
     for d in range(1, NK):
         tk(d).wait_send()
         pk(d).wait_send()
@@ -399,7 +363,6 @@
             pltpu.VMEM((LENGTH, HEAD), bf),
             pltpu.VMEM((LENGTH, HEAD), bf),
             pltpu.VMEM((COLS, OUT), bf),
-            pltpu.VMEM((HEAD, LENGTH), bf),
             pltpu.VMEM((LENGTH, 2 * HEAD), bf),
             pltpu.VMEM((ROWS, LENGTH), f32),
             pltpu.VMEM((ROWS, LENGTH), f32),
@@ -417,12 +380,12 @@
             pltpu.VMEM((NK, SHARE, OUT), bf),
             pltpu.VMEM((NK, SHARE, OUT), bf),
             dma((3,)),
-            dma((NX - 1,)), dma((NX - 1,)),
+            dma((NZ, NX - 1)), dma((NZ, NX - 1)),
             dma((4,)), dma((4,)), dma((4,)), dma((4,)),
             dma((NZ, NX - 1)), dma((NZ, NX - 1)),
             dma((NZ - 1,)), dma((NZ - 1,)),
             dma((NZ - 1,)), dma((NZ - 1,)),
-            dma((NZ,)), dma((NZ,)), dma((NZ,)), dma((NZ,)), dma((NZ,)), dma((NZ,)),
+            dma((NZ, NX - 1)), dma((NZ, NX - 1)),
             dma((NK - 1,)), dma((NK - 1,)), dma((NK - 1,)), dma((NK - 1,)),
         ],
         compiler_params=pltpu.CompilerParams(

time: 85.4 us -> 79.8 us (0.934)
  Pallas kernels: 83.2 us -> 77.5 us
    pallas_call x1, Pallas kernels: 83.2 us -> 77.5 us  [per_device(): pl.pallas_call(kernel, out_shape=jax.ShapeDtypeStruct((SHARE, 2 * OUT), b...]
where the time goes in v3:
time: 79.8 us; the launch traced here: 79.5 us
  Pallas kernels  77.5 us (97%)
  other arithmetic  1.41 us (2%)
    pallas_call x1, Pallas kernels, per_device(): pl.pallas_call(kernel, out_shape=jax.ShapeDtypeStruct((SHARE, 2 * OUT), b...  77.5 us

profile of v3, /device:TPU:1, one launch (start us, length us, event | category | flops | bytes accessed | tf_op | source)
XLA Modules:
  0.0 79.5 jit_solution(3183608155752654684)
XLA Ops:
  0.6 77.5 %shard_map.77 = bf16[64,512]{1,0:T(8,128)(2,1)} custom-call(bf16[16,1024]{1,0:T(8,128)(2,1)} %q_ref.1, bf16[4096,128]{1,0:T(8,128)(2,1)} %k_ref.1, bf16[4096,128]{1,0:T(8,128)(2,1)} %v_ref.1, bf16[1024,256]{1,0:T(8,128)(2,1)} %w_ref.1, s32[16]{0:T(128)} %pos_ref.1, s32[1,512]{1,0:T(1,128)} %bitcast.1), custom_call_target="tpu_custom_call" | custom-call | tf_op jit(solution)/shard_map/pallas_call | solution.py:357
  78.1 1.4 %subtract_convert_fusion = (bf16[64,256]{1,0:T(8,128)(2,1)}, bf16[64,256]{1,0:T(8,128)(2,1)}) fusion(bf16[64,512]{1,0:T(8,128)(2,1)} %shard_map.77), kind=kLoop, calls=%fused_computation | loop fusion | flops 65536 | bytes 131072 | tf_op jit(solution)/shard_map/convert_element_type | solution.py:395

commit v4 on v3

--- a/solution.py
+++ b/solution.py
@@ -190,16 +190,11 @@
     start = seq * LENGTH
     run_of = (run.at[0], run.at[1])
 
-    def attention(a, a_slot, b, b_slot, done=None):
-        if done is not None:
-            for d in range(1, NX):
-                px(done, d).wait_recv()
+    def attention(a, dz, a_slot, b, b_slot, done=None):
         if a is not None:
             for e in (1, 3, 2):
-                fq(order[a], e).wait_recv()
-            if a == 0:
-                hop(1)
-            a_z = (z + order[a]) % NZ
+                fq(dz, e).wait_recv()
+            a_z = (z + dz) % NZ
             q = jnp.concatenate([q_all[a_z, :, h * HEAD : (h + 1) * HEAD] for h in range(HEADS)], axis=0)
             c = q_all[a_z, :, COLS:WIDE].astype(jnp.float32)
             count = (c[:, 0:1] * 4096.0 + c[:, 1:2] * 16.0 + c[:, 2:3]).astype(jnp.int32) - start
@@ -240,8 +235,6 @@
             part[b, :, COLS:WIDE] = spread(tile)
             for d in range(1, NX):
                 px(b, d).start()
-        if done is not None and done > 0:
-            pz(done).start()
 
     def over_x(n):
         outs = [lambda h: part[n, block(x), h * HEAD : (h + 1) * HEAD]]
@@ -252,28 +245,87 @@
             zpart[n, :, h * HEAD : (h + 1) * HEAD] = merged[h]
         zpart[n, :, COLS:WIDE] = spread(log)
 
-    attention(0, 0, None, None)
+    hop(1)
+    attention(0, 0, 0, None, None)
     pairs[...] = jnp.where(
         lax.broadcasted_iota(jnp.int32, (TOKENS, TOKENS), 0) == partner_ref[...], 1.0, 0.0).astype(jnp.bfloat16)
-    attention(None, None, 0, 0)
     loads[2].wait()
-
-    hop(2)
-    attention(1, 1, None, None)
-    attention(2, 0, 1, 1)
-    hop(3)
-    attention(3, 1, 2, 0, 0)
-    hop(4)
-    attention(4, 0, 3, 1, 1)
-    attention(5, 1, 4, 0, 2)
-    attention(6, 0, 5, 1, 3)
-    attention(7, 1, 6, 0, 4)
-    attention(None, None, 7, 1, 5)
-    for n in (NZ - 2, NZ - 1):
-        for d in range(1, NX):
-            px(n, d).wait_recv()
+    for blocks in (part, part_in):
+        blocks[NZ:] = jnp.zeros_like(blocks[NZ:])
+
+    def arrived(n):
+        for e in range(1, NX):
+            px(n, e).wait_recv()
+
+    def two(j, _):
+        older, old = (2 * j + NZ) % (NZ + 2), (2 * j + NZ + 1) % (NZ + 2)
+
+        @pl.when(j == 1)
+        def _():
+            hop(3)
+
+        @pl.when(j > 0)
+        def _():
+            arrived(older)
+
+        attention(2 * j + 1, j + 1 + j // 3, 1, 2 * j, 0, older)
+
+        @pl.when(j == 0)
+        def _():
+            hop(2)
+
+        @pl.when(j == 1)
+        def _():
+            hop(4)
+
+        @pl.when(j == 2)
+        def _():
+            pz(2).start()
+
+        @pl.when(j == 3)
+        def _():
+            pz(4).start()
+
+        @pl.when(j > 0)
+        def _():
+            arrived(old)
+
+        @pl.when(j < 3)
+        def _():
+            attention(2 * j + 2, 7 - j - j // 2, 0, 2 * j + 1, 1, old)
+
+        @pl.when(j == 3)
+        def _():
+            attention(None, None, None, 2 * j + 1, 1, old)
+            pz(5).start()
+
+        @pl.when(j == 1)
+        def _():
+            pz(1).start()
+
+        @pl.when(j == 2)
+        def _():
+            pz(3).start()
+
+        return 0
+
+    lax.fori_loop(0, NZ // 2, two, 0)
+
+    def last(n, _):
+        arrived(n)
         over_x(n)
-        pz(n).start()
+
+        @pl.when(n == NZ - 2)
+        def _():
+            pz(NZ - 2).start()
+
+        @pl.when(n == NZ - 1)
+        def _():
+            pz(NZ - 1).start()
+
+        return 0
+
+    lax.fori_loop(NZ - 2, NZ, last, 0)
 
     for n in range(1, NZ):
         pz(n).wait_recv()
@@ -368,9 +420,9 @@
             pltpu.VMEM((ROWS, LENGTH), f32),
             pltpu.VMEM((2, ROWS, 128), f32),
             pltpu.VMEM((NZ, SLAB, WIDE), bf),
-            pltpu.VMEM((NZ, SLAB, WIDE), bf),
-            pltpu.VMEM((NZ, NX - 1, TOK, WIDE), bf),
-            pltpu.VMEM((NZ, TOK, WIDE), bf),
+            pltpu.VMEM((NZ + 2, SLAB, WIDE), bf),
+            pltpu.VMEM((NZ + 2, NX - 1, TOK, WIDE), bf),
+            pltpu.VMEM((NZ + 2, TOK, WIDE), bf),
             pltpu.VMEM((NZ, TOK, WIDE), bf),
             pltpu.VMEM((NX, CHUNK, COLS), bf),
             pltpu.VMEM((TOKENS, TOKENS), bf),

time: 79.8 us -> 80.9 us (1.014)
  Pallas kernels: 77.5 us -> 78.6 us
    pallas_call x1, Pallas kernels: 77.5 us -> 78.6 us  [per_device(): pl.pallas_call(kernel, out_shape=jax.ShapeDtypeStruct((SHARE, 2 * OUT), b...]
where the time goes in v4:
time: 80.9 us; the launch traced here: 80.7 us
  Pallas kernels  78.6 us (97%)
  other arithmetic  1.41 us (2%)
    pallas_call x1, Pallas kernels, per_device(): pl.pallas_call(kernel, out_shape=jax.ShapeDtypeStruct((SHARE, 2 * OUT), b...  78.6 us

profile of v4, /device:TPU:1, one launch (start us, length us, event | category | flops | bytes accessed | tf_op | source)
XLA Modules:
  0.0 80.7 jit_solution(10728504537058939363)
XLA Ops:
  0.6 78.6 %shard_map.77 = bf16[64,512]{1,0:T(8,128)(2,1)} custom-call(bf16[16,1024]{1,0:T(8,128)(2,1)} %q_ref.1, bf16[4096,128]{1,0:T(8,128)(2,1)} %k_ref.1, bf16[4096,128]{1,0:T(8,128)(2,1)} %v_ref.1, bf16[1024,256]{1,0:T(8,128)(2,1)} %w_ref.1, s32[16]{0:T(128)} %pos_ref.1, s32[1,512]{1,0:T(1,128)} %bitcast.1), custom_call_target="tpu_custom_call" | custom-call | tf_op jit(solution)/shard_map/pallas_call | solution.py:409
  79.3 1.4 %subtract_convert_fusion = (bf16[64,256]{1,0:T(8,128)(2,1)}, bf16[64,256]{1,0:T(8,128)(2,1)}) fusion(bf16[64,512]{1,0:T(8,128)(2,1)} %shard_map.77), kind=kLoop, calls=%fused_computation | loop fusion | flops 65536 | bytes 131072 | tf_op jit(solution)/shard_map/convert_element_type | solution.py:447

commit v5 on v4

--- a/solution.py
+++ b/solution.py
@@ -252,60 +252,53 @@
     loads[2].wait()
     for blocks in (part, part_in):
         blocks[NZ:] = jnp.zeros_like(blocks[NZ:])
+    hop(2)
 
     def arrived(n):
         for e in range(1, NX):
             px(n, e).wait_recv()
 
     def two(j, _):
-        older, old = (2 * j + NZ) % (NZ + 2), (2 * j + NZ + 1) % (NZ + 2)
+        older, old = (2 * j + NZ) % (NZ + 3), (2 * j + NZ + 1) % (NZ + 3)
 
         @pl.when(j == 1)
         def _():
+            hop(4)
+
+        @pl.when(j > 1)
+        def _():
+            arrived(older)
+
+        attention(2 * j + 1, j + 1 + j // 3, 1, 2 * j, 0, older)
+
+        @pl.when(j == 0)
+        def _():
             hop(3)
 
+        @pl.when(j == 2)
+        def _():
+            pz(1).start()
+
+        @pl.when(j == 3)
+        def _():
+            pz(3).start()
+
         @pl.when(j > 0)
         def _():
-            arrived(older)
-
-        attention(2 * j + 1, j + 1 + j // 3, 1, 2 * j, 0, older)
-
-        @pl.when(j == 0)
-        def _():
-            hop(2)
-
-        @pl.when(j == 1)
-        def _():
-            hop(4)
+            arrived(old)
+
+        @pl.when(j < 3)
+        def _():
+            attention(2 * j + 2, 7 - j - j // 2, 0, 2 * j + 1, 1, old)
+
+        @pl.when(j == 3)
+        def _():
+            attention(None, None, None, 2 * j + 1, 1, old)
+            pz(4).start()
 
         @pl.when(j == 2)
         def _():
             pz(2).start()
-
-        @pl.when(j == 3)
-        def _():
-            pz(4).start()
-
-        @pl.when(j > 0)
-        def _():
-            arrived(old)
-
-        @pl.when(j < 3)
-        def _():
-            attention(2 * j + 2, 7 - j - j // 2, 0, 2 * j + 1, 1, old)
-
-        @pl.when(j == 3)
-        def _():
-            attention(None, None, None, 2 * j + 1, 1, old)
-            pz(5).start()
-
-        @pl.when(j == 1)
-        def _():
-            pz(1).start()
-
-        @pl.when(j == 2)
-        def _():
-            pz(3).start()
 
         return 0
 
@@ -315,17 +308,15 @@
         arrived(n)
         over_x(n)
 
-        @pl.when(n == NZ - 2)
-        def _():
-            pz(NZ - 2).start()
-
-        @pl.when(n == NZ - 1)
-        def _():
-            pz(NZ - 1).start()
+        for m in range(NZ - 3, NZ):
+
+            @pl.when(n == m)
+            def _():
+                pz(m).start()
 
         return 0
 
-    lax.fori_loop(NZ - 2, NZ, last, 0)
+    lax.fori_loop(NZ - 3, NZ, last, 0)
 
     for n in range(1, NZ):
         pz(n).wait_recv()
@@ -420,9 +411,9 @@
             pltpu.VMEM((ROWS, LENGTH), f32),
             pltpu.VMEM((2, ROWS, 128), f32),
             pltpu.VMEM((NZ, SLAB, WIDE), bf),
-            pltpu.VMEM((NZ + 2, SLAB, WIDE), bf),
-            pltpu.VMEM((NZ + 2, NX - 1, TOK, WIDE), bf),
-            pltpu.VMEM((NZ + 2, TOK, WIDE), bf),
+            pltpu.VMEM((NZ + 3, SLAB, WIDE), bf),
+            pltpu.VMEM((NZ + 3, NX - 1, TOK, WIDE), bf),
+            pltpu.VMEM((NZ + 3, TOK, WIDE), bf),
             pltpu.VMEM((NZ, TOK, WIDE), bf),
             pltpu.VMEM((NX, CHUNK, COLS), bf),
             pltpu.VMEM((TOKENS, TOKENS), bf),

time: 80.9 us -> 73.4 us (0.907)
  Pallas kernels: 78.6 us -> 71.2 us
    pallas_call x1, Pallas kernels: 78.6 us -> 71.2 us  [per_device(): pl.pallas_call(kernel, out_shape=jax.ShapeDtypeStruct((SHARE, 2 * OUT), b...]
where the time goes in v5:
time: 73.4 us; the launch traced here: 73.2 us
  Pallas kernels  71.2 us (97%)
  other arithmetic  1.41 us (2%)
    pallas_call x1, Pallas kernels, per_device(): pl.pallas_call(kernel, out_shape=jax.ShapeDtypeStruct((SHARE, 2 * OUT), b...  71.2 us

profile of v5, /device:TPU:1, one launch (start us, length us, event | category | flops | bytes accessed | tf_op | source)
XLA Modules:
  0.0 73.2 jit_solution(12717244413233654650)
XLA Ops:
  0.6 71.2 %shard_map.77 = bf16[64,512]{1,0:T(8,128)(2,1)} custom-call(bf16[16,1024]{1,0:T(8,128)(2,1)} %q_ref.1, bf16[4096,128]{1,0:T(8,128)(2,1)} %k_ref.1, bf16[4096,128]{1,0:T(8,128)(2,1)} %v_ref.1, bf16[1024,256]{1,0:T(8,128)(2,1)} %w_ref.1, s32[16]{0:T(128)} %pos_ref.1, s32[1,512]{1,0:T(1,128)} %bitcast.1), custom_call_target="tpu_custom_call" | custom-call | tf_op jit(solution)/shard_map/pallas_call | solution.py:400
  71.8 1.4 %subtract_convert_fusion = (bf16[64,256]{1,0:T(8,128)(2,1)}, bf16[64,256]{1,0:T(8,128)(2,1)}) fusion(bf16[64,512]{1,0:T(8,128)(2,1)} %shard_map.77), kind=kLoop, calls=%fused_computation | loop fusion | flops 65536 | bytes 131072 | tf_op jit(solution)/shard_map/convert_element_type | solution.py:438

commit v6 on v5

--- a/solution.py
+++ b/solution.py
@@ -77,7 +77,7 @@
 def kernel(
     q_ref, k_ref, v_ref, w_ref, pos_ref, partner_ref, total_ref,
     k_buf, v_buf, w_buf, vp, s0, s1, run, q_all, part, part_in, zpart, z_in, att, pairs, terms, t_out, t_in, p_out, p_in,
-    local_sem, fq_send, fq_recv, up_send, up_recv, down_send, down_recv, px_send, px_recv, pz_send, pz_recv,
+    local_sem, fq_send, fq_recv, side_send, side_recv, up_send, up_recv, down_send, down_recv, px_send, px_recv, pz_send, pz_recv,
     az_send, az_recv, ax_send, ax_recv, t_send, t_recv, p_send, p_recv,
 ):
     seq = lax.axis_index("seq")
@@ -142,6 +142,10 @@
         here = q_all.at[(z + dz) % NZ, block(x)]
         return remote(here, here, fq_send.at[dz, e - 1], fq_recv.at[dz, e - 1], x_peer(e))
 
+    def side(e, way):
+        here = q_all.at[z, block((x + e) % NX)]
+        return remote(here, here, side_send.at[way, e - 1], side_recv.at[way, e - 1], z_peer((1, NZ - 1)[way]))
+
     def hop(k):
         up(k).wait_recv()
         if k < NZ // 2:
@@ -150,8 +154,9 @@
         if k + 1 < NZ // 2:
             down(k + 1).start()
         for e in (1, 3, 2):
-            fq(NZ - k, e).start()
-            if k < NZ // 2:
+            if k > 1:
+                fq(NZ - k, e).start()
+            if 1 < k < NZ // 2:
                 fq(k, e).start()
 
     def px(n, d):
@@ -192,8 +197,6 @@
 
     def attention(a, dz, a_slot, b, b_slot, done=None):
         if a is not None:
-            for e in (1, 3, 2):
-                fq(dz, e).wait_recv()
             a_z = (z + dz) % NZ
             q = jnp.concatenate([q_all[a_z, :, h * HEAD : (h + 1) * HEAD] for h in range(HEADS)], axis=0)
             c = q_all[a_z, :, COLS:WIDE].astype(jnp.float32)
@@ -245,6 +248,10 @@
             zpart[n, :, h * HEAD : (h + 1) * HEAD] = merged[h]
         zpart[n, :, COLS:WIDE] = spread(log)
 
+    for e in (1, 3, 2):
+        fq(0, e).wait_recv()
+        side(NX - e, 0).start()
+        side(NX - e, 1).start()
     hop(1)
     attention(0, 0, 0, None, None)
     pairs[...] = jnp.where(
@@ -269,6 +276,16 @@
         def _():
             arrived(older)
 
+        @pl.when(j == 0)
+        def _():
+            for e in range(1, NX):
+                side(e, 1).wait_recv()
+
+        @pl.when(j > 0)
+        def _():
+            for e in range(1, NX):
+                fq(j + 1 + j // 3, e).wait_recv()
+
         attention(2 * j + 1, j + 1 + j // 3, 1, 2 * j, 0, older)
 
         @pl.when(j == 0)
@@ -286,6 +303,16 @@
         @pl.when(j > 0)
         def _():
             arrived(old)
+
+        @pl.when(j == 0)
+        def _():
+            for e in range(1, NX):
+                side(e, 0).wait_recv()
+
+        @pl.when(j * (3 - j) > 0)
+        def _():
+            for e in range(1, NX):
+                fq(7 - j - j // 2, e).wait_recv()
 
         @pl.when(j < 3)
         def _():
@@ -377,9 +404,13 @@
 
     for n in range(NZ):
         for e in range(1, NX):
-            fq(n, e).wait_send()
+            if n not in (1, NZ - 1):
+                fq(n, e).wait_send()
             px(n, e).wait_send()
             ax(n, e).wait_send()
+    for e in range(1, NX):
+        side(e, 0).wait_send()
+        side(e, 1).wait_send()
     for k in range(1, NZ // 2 + 1):
         up(k).wait_send()
         if k < NZ // 2:
@@ -424,6 +455,7 @@
             pltpu.VMEM((NK, SHARE, OUT), bf),
             dma((3,)),
             dma((NZ, NX - 1)), dma((NZ, NX - 1)),
+            dma((2, NX - 1)), dma((2, NX - 1)),
             dma((4,)), dma((4,)), dma((4,)), dma((4,)),
             dma((NZ, NX - 1)), dma((NZ, NX - 1)),
             dma((NZ - 1,)), dma((NZ - 1,)),

time: 73.4 us -> 73 us (level)
  no operation moved by 1% of the time
where the time goes in v6:
time: 73 us; the launch traced here: 72.8 us
  Pallas kernels  70.7 us (97%)
  other arithmetic  1.41 us (2%)
    pallas_call x1, Pallas kernels, per_device(): pl.pallas_call(kernel, out_shape=jax.ShapeDtypeStruct((SHARE, 2 * OUT), b...  70.7 us

profile of v6, /device:TPU:1, one launch (start us, length us, event | category | flops | bytes accessed | tf_op | source)
XLA Modules:
  0.0 72.8 jit_solution(5982275134920728541)
XLA Ops:
  0.6 70.7 %shard_map.77 = bf16[64,512]{1,0:T(8,128)(2,1)} custom-call(bf16[16,1024]{1,0:T(8,128)(2,1)} %q_ref.1, bf16[4096,128]{1,0:T(8,128)(2,1)} %k_ref.1, bf16[4096,128]{1,0:T(8,128)(2,1)} %v_ref.1, bf16[1024,256]{1,0:T(8,128)(2,1)} %w_ref.1, s32[16]{0:T(128)} %pos_ref.1, s32[1,512]{1,0:T(1,128)} %bitcast.1), custom_call_target="tpu_custom_call" | custom-call | tf_op jit(solution)/shard_map/pallas_call | solution.py:431
  71.4 1.4 %subtract_convert_fusion = (bf16[64,256]{1,0:T(8,128)(2,1)}, bf16[64,256]{1,0:T(8,128)(2,1)}) fusion(bf16[64,512]{1,0:T(8,128)(2,1)} %shard_map.77), kind=kLoop, calls=%fused_computation | loop fusion | flops 65536 | bytes 131072 | tf_op jit(solution)/shard_map/convert_element_type | solution.py:470
